TPU v7x, 768 devices: a whole 4x8x12 slice. The times are simulated.
768 devices in a mesh: row: 96 (over x, z, core), col: 8 (over y).
Axes of the slice: x: 4, y: 8, z: 12, core: 2. Of those that a mesh axis runs over, the one named last changes fastest.
Arguments:
- ocean: bfloat16 [96, 8, 12, 8192], P('row', 'col'), may hold values from -6 to 6
- land: int32 [96, 8, 8192], P('row', 'col'), may hold values 0 or 1
- weights: bfloat16 [96, 8, 24, 256, 128], P('row', 'col'), may hold values from -0.5 to 0.5
- col_map: int32 [96, 8, 24, 256], P('row', 'col'), may hold values from 0 to 8191
- row_map: int32 [96, 8, 24, 128], P('row', 'col'), may hold values from 0 to 2047
- dest: int32 [96, 8, 24, 1], P('row', 'col'), may hold values from 0 to 8; in each aligned block of 24 rows (0 to 23, 24 to 47, ..., all dimensions but the last counted through in order) at most 4 rows name the same one
- counts: int32 [96, 8], P('row', 'col'), may hold values from 12 to 24, as said below
- kappa: float32 [1536, 1024], P('row', 'col'), may hold values from 0.02 to 0.15
Outputs:
- smoothed: float32 [12, 1536, 1024], P(None, 'row', 'col')
Inputs may be any that keep to these rules, and one draw needn't show every extreme that they name: `dest`: destination d of a block names atmosphere band (own band + d // 3 - 1) and tile column (own column + d % 3 - 1) mod 8; among the 24 blocks of one ocean tile at most 4 have the same d. Blocks numbered counts or higher are padding and their weights are to be ignored.
All inputs are finite; a program needn't handle non-finite values. No bound on the sum of `land` on one device may be relied on, other than what follows from the above.
Results may differ from a plain program's by a relative error of at most 0.00035.
Values sent between devices are 32-bit elements; how exact they have to be, the bound alone decides.
No kernel may reach another device: no remote copies, remote signals or barrier semaphores. Data moves between devices by JAX's collectives and lax.ppermute only.
A program may use at most 64 MiB of HBM per device.

v0:
```python
import functools

import jax
import jax.numpy as jnp
from jax import lax
from jax.experimental import pallas as pl
from jax.experimental.pallas import tpu as pltpu
from jax.sharding import PartitionSpec as P

F, AY, AX, OC, NBLK, BC, BR = 12, 16, 128, 8192, 24, 256, 128
MIX = (1, 0)
NT = (((1,), (1,)), ((), ()))


def split2(x):
    hi = x.astype(jnp.bfloat16)
    return hi, (x - hi.astype(jnp.float32)).astype(jnp.bfloat16)


def remap_kernel(side_ref, counts_in, dest_in, ocean_in, land_in, weights_in, col_in, row_in, kappa_in,
                 sent_out, kept_out, mid_out, dest_ref, counts_ref, ocean_ref, land_ref, weight_ref, col_ref, row_ref, kappa_ref,
                 fields_ref, table_ref, rows_ref, partial_ref, tiles_ref, raw_ref, strips_ref, extra_ref, used_ref, sems, out_sems, *, ga, gb):
    f32, bf16, i32 = jnp.float32, jnp.bfloat16, jnp.int32
    pairs = ((land_in, land_ref), (ocean_in.at[0, 0], ocean_ref), (col_in.at[0, 0], col_ref), (weights_in.at[0, 0], weight_ref),
             (counts_in, counts_ref), (row_in.at[0, 0], row_ref), (dest_in, dest_ref), (kappa_in, kappa_ref))
    copies = [pltpu.make_async_copy(a, b, sems.at[i]) for i, (a, b) in enumerate(pairs)]
    for copy in copies:
        copy.start()
    tiles_ref[...] = jnp.zeros_like(tiles_ref)
    raw_ref[...] = jnp.zeros_like(raw_ref)
    for d in range(9):
        used_ref[d] = 0
    copies[0].wait()
    copies[1].wait()
    sea = land_ref[...].astype(f32)
    high = OC // 128
    fields_ref[0:8, :] = ocean_ref[0:8, :].astype(f32) * sea
    fields_ref[8:12, :] = ocean_ref[8:12, :].astype(f32) * sea
    fields_ref[12:16, :] = jnp.zeros((4, OC), f32)
    low8 = fields_ref[8:16, :]
    down8 = pltpu.roll(low8, 4, 0)
    blocks = OC // BC
    cut = lambda a, h: a[:, h * BC:(h + 1) * BC]
    upper = fields_ref[0:8, :]
    rows_ref[0:8 * blocks, :] = jnp.concatenate([cut(upper, h) for h in range(blocks)], 0).astype(bf16)
    rows_ref[8 * blocks:12 * blocks, :] = jnp.concatenate(
        [cut(low8, 2 * p) + cut(down8, 2 * p + 1) for p in range(blocks // 2)], 0).astype(bf16)
    for p in range(high // 2):
        table_ref[:, p * 128:(p + 1) * 128] = low8[:, 256 * p:256 * p + 128] + down8[:, 256 * p + 128:256 * p + 256]
    for copy in copies[2:]:
        copy.wait()
    count = counts_ref[0]
    odd = (lax.broadcasted_iota(i32, (8, 128), 0) >= 4).astype(i32)

    def finish(b, up, down):
        picked = jnp.concatenate([up, down], 0).astype(bf16)
        value = jnp.dot(picked, weight_ref[b], preferred_element_type=f32)
        partial_ref[b] = jnp.where(b < count, value, 0.0)

    cells = lax.broadcasted_iota(i32, (BC, BC), 0)
    odd2 = (lax.broadcasted_iota(i32, (8, BC), 0) >= 4).astype(i32)

    def pick_dot(b):
        col = col_ref[pl.ds(b, 1), :]
        low = jnp.bitwise_and(col, BC - 1)
        hi = jnp.right_shift(col, 8)
        onehot = (cells == low).astype(f32).astype(bf16)
        got = jnp.dot(rows_ref[...], onehot, preferred_element_type=f32)
        hi8 = jnp.broadcast_to(hi, (8, BC))
        up = jnp.zeros((8, BC), f32)
        for h in range(blocks):
            up = jnp.where(hi8 == h, got[8 * h:8 * h + 8], up)
        pair = hi8 - odd2
        down = jnp.zeros((8, BC), f32)
        for p in range(blocks // 2):
            down = jnp.where(pair == 2 * p, got[8 * (blocks + p):8 * (blocks + p) + 8], down)
        down = down + pltpu.roll(down, 4, 0)
        finish(b, up, down)

    def pick(b):
        ups, downs = [], []
        for t in range(BC // 128):
            col = jnp.broadcast_to(col_ref[pl.ds(b, 1), :][:, 128 * t:128 * t + 128], (8, 128))
            low = jnp.bitwise_and(col, 127)
            hi8 = jnp.right_shift(col, 7)
            up = jnp.zeros((8, 128), f32)
            for h in range(high):
                got = jnp.take_along_axis(fields_ref[0:8, 128 * h:128 * h + 128], low, 1)
                up = jnp.where(hi8 == h, got, up)
            pair = hi8 - odd
            down = jnp.zeros((8, 128), f32)
            for p in range(high // 2):
                got = jnp.take_along_axis(table_ref[:, 128 * p:128 * p + 128], low, 1)
                down = jnp.where(pair == 2 * p, got, down)
            ups.append(up)
            downs.append(down + pltpu.roll(down, 4, 0))
        up = jnp.concatenate(ups, 1)
        down = jnp.concatenate(downs, 1)
        finish(b, up, down)

    def groups(n, one):
        def step(i, carry):
            for j in range(n):
                (one if MIX[j % len(MIX)] else pick_dot)(i * n + j)
            return carry
        lax.fori_loop(0, NBLK // n, step, 0)

    groups(ga, pick)
    lanes = lax.broadcasted_iota(i32, (AX, BR), 0)
    rows16 = lax.broadcasted_iota(i32, (AY, BR), 0)

    def place(b):
        cell = row_ref[pl.ds(b, 1), :]
        x = jnp.bitwise_and(cell, AX - 1)
        y = jnp.right_shift(cell, 7)
        at_x = (lanes == x).astype(f32).astype(bf16)
        at_y = rows16 == y
        value = partial_ref[b]
        head = value.astype(bf16).astype(f32)
        tail = value - head
        spread = lambda v: jnp.concatenate(
            [jnp.where(at_y, v[f:f + 1, :], 0.0) for f in range(F)], 0).astype(bf16)
        left = jnp.concatenate([spread(head), spread(tail)], 1)
        right = jnp.concatenate([at_x, at_x], 1)
        return lax.dot_general(left, right, NT, preferred_element_type=f32)

    halves = lax.broadcasted_iota(i32, (8, BR), 0) // 4

    def keep_block(b, d, dc, band):
        live = (b < count).astype(i32)
        at = used_ref[d]
        used_ref[d] = at + live
        wanted = jnp.logical_and(b < count, dc != 1)
        to = lax.div(dc, 2)
        slot = jnp.where(wanted, 4 * band + at, 12)
        raw_ref[to, jnp.where(wanted, slot, 20)] = partial_ref[b, 0:8]
        pair = jnp.where(wanted, 12 + lax.div(slot, 2), 21)
        tail = partial_ref[b, 8:16]
        raw_ref[to, pair] = jnp.where(halves == lax.rem(slot, 2), tail, raw_ref[to, pair])
        raw_ref[to, 18 + lax.div(slot, 8), pl.ds(lax.rem(slot, 8), 1), :] = row_ref[pl.ds(b, 1), :].astype(f32)

    def place_group(i, carry):
        got = [place(i * gb + j) for j in range(gb)]
        for j in range(gb):
            d = dest_ref[i * gb + j]
            dc, band = lax.rem(d, 3), lax.div(d, 3)
            tiles_ref[3 * dc + band] = tiles_ref[3 * dc + band] + got[j]
            keep_block(i * gb + j, d, dc, band)
        return carry

    lax.fori_loop(0, NBLK // gb, place_group, 0)

    side = side_ref[0]
    outs = []

    def out(source, target):
        outs.append(pltpu.make_async_copy(source, target, out_sems.at[len(outs)]))
        outs[-1].start()

    main = F * AY
    out(raw_ref.at[1 - side, pl.ds(0, 20)], sent_out.at[pl.ds(0, 20)])
    out(raw_ref.at[side, pl.ds(0, 20)], kept_out.at[pl.ds(0, 20)])
    out(tiles_ref.at[pl.ds(3, 3)], mid_out.at[:, 0:main])
    er = lax.broadcasted_iota(i32, (16, AX), 0)
    ec = lax.broadcasted_iota(i32, (16, AX), 1)
    edge = (ec == jnp.where(er < 8, er, er + AX - 16)).astype(f32).astype(bf16)
    edge2 = jnp.concatenate([edge, edge], 1)
    kappa = kappa_ref[...]
    extra_ref[...] = jnp.zeros_like(extra_ref)
    extra_ref[1] = kappa
    out(extra_ref, mid_out.at[:, main:main + AY])
    for band in range(3):
        for dc in range(3):
            tile = jnp.concatenate([tiles_ref[3 * dc + band], kappa if 3 * dc + band == 4 else jnp.zeros((AY, AX), f32)], 0)
            hi, lo = split2(tile)
            strip = lax.dot_general(edge2, jnp.concatenate([hi, lo], 1), NT, preferred_element_type=f32)
            first = strip[:, 0:128]
            second = jnp.concatenate([strip[:, 128:], jnp.zeros((16, 256 - 13 * AY), f32)], 1)
            west = (first[0:8], second[0:8])
            east = (first[8:16], second[8:16])

            def put(to, row, strip):
                strips_ref[to, 6 * band + row] = strip[0]
                strips_ref[to, 6 * band + row + 1] = strip[1]

            if dc == 1:
                put(1, 0, east)
                put(0, 0, west)
            elif dc == 2:
                put(1, 2, east)
                put(1, 4, west)
            else:
                put(0, 2, west)
                put(0, 4, east)
    out(strips_ref.at[1 - side], sent_out.at[pl.ds(20, 18)])
    out(strips_ref.at[side], kept_out.at[pl.ds(20, 18)])
    for copy in outs:
        copy.wait()


def remap(side, dest, counts, ocean, land, weights, col_map, row_map, kappa, ga=12, gb=24):
    f32 = jnp.float32
    return pl.pallas_call(
        functools.partial(remap_kernel, ga=ga, gb=gb),
        out_shape=(jax.ShapeDtypeStruct((38, 8, 128), f32), jax.ShapeDtypeStruct((38, 8, 128), f32), jax.ShapeDtypeStruct((3, 208, 128), f32)),
        in_specs=[pl.BlockSpec(memory_space=pltpu.SMEM)] + [pl.BlockSpec(memory_space=pltpu.HBM)] * 8,
        out_specs=[pl.BlockSpec(memory_space=pl.ANY)] * 3,
        scratch_shapes=[
            pltpu.SMEM((NBLK,), jnp.int32),
            pltpu.SMEM((1,), jnp.int32),
            pltpu.VMEM((F, OC), jnp.bfloat16),
            pltpu.VMEM((1, OC), jnp.int32),
            pltpu.VMEM((NBLK, BC, BR), jnp.bfloat16),
            pltpu.VMEM((NBLK, BC), jnp.int32),
            pltpu.VMEM((NBLK, BR), jnp.int32),
            pltpu.VMEM((AY, AX), f32),
            pltpu.VMEM((16, OC), f32),
            pltpu.VMEM((8, OC // 2), f32),
            pltpu.VMEM((384, BC), jnp.bfloat16),
            pltpu.VMEM((NBLK, 16, BR), f32),
            pltpu.VMEM((9, F * AY, AX), f32),
            pltpu.VMEM((2, 22, 8, BR), f32),
            pltpu.VMEM((2, 18, 8, AX), f32),
            pltpu.VMEM((3, AY, AX), f32),
            pltpu.SMEM((9,), jnp.int32),
            pltpu.SemaphoreType.DMA((8,)),
            pltpu.SemaphoreType.DMA((6,)),
        ],
        compiler_params=pltpu.CompilerParams(vmem_limit_bytes=32 * 1024 * 1024),
    )(side, counts, *[pltpu.with_memory_space_constraint(v, pltpu.HBM) for v in (dest, ocean, land, weights, col_map, row_map, kappa)])


def collect_kernel(place_ref, got_ref, mid_ref, far_ref, beside_ref, sent_ref, kept_ref, total_ref):
    f32, bf16, i32 = jnp.float32, jnp.bfloat16, jnp.int32
    core, side = place_ref[0], place_ref[1]
    main = 13 * AY
    total_ref[:, 0:main] = jnp.zeros((4, main, AX), f32)
    total_ref[pl.ds(core, 3), 0:main] = mid_ref[...]
    for q in range(4):
        for i in range(2):
            at = main + 8 * i
            total_ref[q, at:at + 8] = (got_ref[side, 40 + 2 * q + i] + far_ref[q, 8 * i:8 * i + 8]
                                       + beside_ref[q, 8 * i:8 * i + 8])
    lanes = lax.broadcasted_iota(i32, (AX, BR), 0)
    rows16 = lax.broadcasted_iota(i32, (AY, BR), 0)

    def factors(t, slot):
        base = 20 * t
        last = 4 * (slot % 2)
        value = jnp.concatenate([got_ref[side, base + slot], got_ref[side, base + 12 + slot // 2][last:last + 4]], 0)
        cell = got_ref[side, base + 18 + slot // 8][slot % 8:slot % 8 + 1].astype(i32)
        at_x = (lanes == jnp.bitwise_and(cell, AX - 1)).astype(f32).astype(bf16)
        at_y = rows16 == jnp.right_shift(cell, 7)
        head = value.astype(bf16).astype(f32)
        tail = value - head
        spread = lambda v: jnp.concatenate([jnp.where(at_y, v[f:f + 1, :], 0.0) for f in range(F)], 0).astype(bf16)
        return jnp.concatenate([spread(head), spread(tail)], 1), jnp.concatenate([at_x, at_x], 1)

    for q in range(4):
        slots = [(t, 4 * (q - t) + k) for t in range(2) if 0 <= q - t < 3 for k in range(4)]
        added = jnp.zeros((F * AY, AX), f32)
        for t, slot in slots:
            left, right = factors(t, slot)
            added = added + lax.dot_general(left, right, NT, preferred_element_type=f32)
        total_ref[q, 0:F * AY] = total_ref[q, 0:F * AY] + added
    kept_ref[...] = total_ref[pl.ds(2 * core, 2)]
    sent_ref[...] = total_ref[pl.ds(2 - 2 * core, 2)]


def collect(place, got, mid, far, beside):
    vm = pl.BlockSpec(memory_space=pltpu.VMEM)
    half = jax.ShapeDtypeStruct((2, 224, AX), jnp.float32)
    return pl.pallas_call(
        collect_kernel,
        out_shape=(half, half),
        in_specs=[pl.BlockSpec(memory_space=pltpu.SMEM), vm, vm, vm, vm],
        out_specs=(vm, vm),
        scratch_shapes=[pltpu.VMEM((4, 224, AX), jnp.float32)],
        compiler_params=pltpu.CompilerParams(vmem_limit_bytes=16 * 1024 * 1024),
    )(place, got, mid, far, beside)


SWEEPS = 3


def smooth_kernel(inside_ref, own_ref, top_ref, bottom_ref, out_ref, side_ref, main_ref, halo_ref):
    f32, i32 = jnp.float32, jnp.int32
    wide = 2 * AX
    tall = AY + 16
    strip = lambda ref, at: jnp.concatenate([ref[at:at + 8, :], ref[at + 8:at + 16, :]], 1)
    below = lax.rem(lax.broadcasted_iota(i32, (8, wide), 1), AY) < 8
    ends = lambda at: jnp.where(below, strip(bottom_ref, at), strip(top_ref, at))
    for slot, (west, east) in enumerate(((strip(own_ref, 13 * AY), strip(own_ref, 13 * AY + 16)),
                                         (ends(13 * 8), ends(13 * 8 + 16)))):
        block = jnp.concatenate([east, jnp.zeros((AX - 16, wide), f32), west], 0)
        side_ref[slot, 0:AX] = block[:, :AX].T
        side_ref[slot, AX:wide] = block[:, AX:].T

    rows = lax.broadcasted_iota(i32, (tall, AX), 0)
    lane = lax.broadcasted_iota(i32, (24, AX), 1)
    inside = jnp.logical_and(jnp.logical_or(rows >= 8, inside_ref[0] == 1),
                             jnp.logical_or(rows < 8 + AY, inside_ref[1] == 1))
    for f in range(F + 1):
        keep = (lambda v, lo, hi: jnp.where(inside[lo:hi], v, 0.0)) if f < F else (lambda v, lo, hi: v)
        main_ref[f, 0:8] = keep(top_ref[8 * f:8 * f + 8], 0, 8)
        main_ref[f, 8:8 + AY] = own_ref[AY * f:AY * f + AY]
        main_ref[f, 8 + AY:tall] = keep(bottom_ref[8 * f:8 * f + 8], 8 + AY, tall)
        halo_ref[f, 0:8] = keep(side_ref[1, AY * f + 8:AY * f + 16], 0, 8)
        halo_ref[f, 8:8 + AY] = side_ref[0, AY * f:AY * f + AY]
        halo_ref[f, 8 + AY:tall] = keep(side_ref[1, AY * f:AY * f + 8], 8 + AY, tall)

    def lap(ref, f, lo, n, own_rolls, other_rolls):
        at = lambda by: ref[f, lo + by:lo + by + n]
        size = lane[:n]
        turned = {by: jnp.where(size >= by if by > 0 else size < AX + by, own_rolls[by], other_rolls[by])
                  for by in (1, -1, 2, -2)}
        near = (at(-1) + at(1)) + (turned[1] + turned[-1])
        far = (at(-2) + at(2)) + (turned[2] + turned[-2])
        return 4.0 / 3.0 * near - 1.0 / 12.0 * far - 5.0 * at(0)

    for sweep in range(SWEEPS):
        last = sweep == SWEEPS - 1
        lo, n = (8, AY) if last else (4, 24)
        kappa_main, kappa_halo = main_ref[F, lo:lo + n], halo_ref[F, lo:lo + n]
        seen = inside[4:28]
        for f in range(F):
            u, v = main_ref[f, lo:lo + n], halo_ref[f, lo:lo + n]
            u_rolls = {by: pltpu.roll(u, by % AX, 1) for by in (1, -1, 2, -2)}
            v_rolls = {by: pltpu.roll(v, by % AX, 1) for by in (1, -1, 2, -2)}
            u = u + kappa_main * lap(main_ref, f, lo, n, u_rolls, v_rolls)
            if last:
                out_ref[f] = u
            else:
                v = v + kappa_halo * lap(halo_ref, f, lo, n, v_rolls, u_rolls)
                main_ref[f, lo:lo + n] = jnp.where(seen, u, 0.0)
                halo_ref[f, lo:lo + n] = jnp.where(seen, v, 0.0)


def smooth(inside, own, top, bottom):
    vm = pl.BlockSpec(memory_space=pltpu.VMEM)
    return pl.pallas_call(
        smooth_kernel,
        out_shape=jax.ShapeDtypeStruct((F, AY, AX), jnp.float32),
        in_specs=[pl.BlockSpec(memory_space=pltpu.SMEM), vm, vm, vm],
        out_specs=vm,
        scratch_shapes=[
            pltpu.VMEM((2, 2 * AX, AX), jnp.float32),
            pltpu.VMEM((F + 1, AY + 16, AX), jnp.float32),
            pltpu.VMEM((F + 1, AY + 16, AX), jnp.float32),
        ],
        compiler_params=pltpu.CompilerParams(vmem_limit_bytes=16 * 1024 * 1024),
    )(inside, own, top, bottom)


def partners(n_row, n_col):
    at = lambda r, c: (r % n_row) * n_col + c % n_col
    chip = [[at(2 * k, c), at(2 * k + 1, c)] for k in range(n_row // 2) for c in range(n_col)]
    beside = [[at(r, c), at(r, c + 1)] for r in range(n_row) for c in range(r % 2, n_col, 2)]
    bands = [[at(2 * k + 1, c), at(2 * k + 2, c)] for k in range(n_row // 2 - 1) for c in range(n_col)]
    bands += [[at(r, c), at(r, c + 1)] for r in (0, n_row - 1) for c in range(0, n_col, 2)]
    beyond = []
    for r in range(n_row):
        for c in range(n_col):
            step = 2 if (r + c) % 2 == 0 else -2
            beyond.append((at(r, c), at(r ^ 1, c + step)))
    return chip, beside, bands, beyond


def per_device(ocean, land, weights, col_map, row_map, dest, counts, kappa):
    both = ("row", "col")
    n_row, n_col = lax.axis_size("row"), lax.axis_size("col")
    chip, beside, bands, beyond = partners(n_row, n_col)
    row, col = lax.axis_index("row"), lax.axis_index("col")
    core = row % 2
    first = core == 0
    ahead = (row + col) % 2 == 0
    side = jnp.where(ahead, 1, 0).astype(jnp.int32)
    swap = lambda value, groups, place: lax.dynamic_index_in_dim(
        lax.all_gather(value, both, axis_index_groups=groups), place, 0, keepdims=False)
    take = lambda value, place: lax.dynamic_index_in_dim(value, place, 0, keepdims=False)
    part = lambda value, start, size, dim: lax.dynamic_slice_in_dim(value, start, size, dim)

    sent, mine, mid = remap(side.reshape(1), dest.reshape(NBLK), counts.reshape(1), ocean, land.reshape(1, OC), weights, col_map, row_map, kappa)
    other = swap(sent, chip, 1 - core)
    lower, upper = jnp.where(first, mine, other), jnp.where(first, other, mine)
    lift = lambda value, before: jnp.pad(value[20:].reshape(3, 48, AX), ((before, 1 - before), (0, 0), (0, 0)))
    strips = lift(lower, 0) + lift(upper, 1)
    far = lax.ppermute(strips[:, 16:32], both, beyond)
    near = lax.all_gather(jnp.concatenate([lower[:20], upper[:20], strips[:, 0:16].reshape(8, 8, AX)], 0),
                          both, axis_index_groups=beside)
    sent, mine = collect(jnp.stack([core, side]).astype(jnp.int32), near, mid, far, strips[:, 32:48])
    other = swap(sent, chip, 1 - core)
    east = jnp.where(ahead, mine[:, 208:], other[:, 208:])
    west = jnp.where(ahead, other[:, 208:], mine[:, 208:])
    main = mine[:, :208] + other[:, :208]
    half = lambda value, start: part(value[:208].reshape(13, AY, AX), start, 8, 1).reshape(104, AX)
    edges = jnp.concatenate([west, east], 1)
    mine_main, mine_edges = take(main, 1 - core), take(edges, 1 - core)
    out_main, out_edges = take(main, core), take(edges, core)
    sent = jnp.concatenate([out_main, out_edges, half(mine_main, 8 * core), mine_edges], 0)
    got = swap(sent, bands, core)
    outer = jnp.logical_or(row == 0, row == n_row - 1)
    got = jnp.where(outer, 0.0, got)
    own = jnp.concatenate([mine_main, mine_edges], 0) + got[:240]
    outside = jnp.concatenate([half(out_main, 8 - 8 * core), out_edges], 0) + got[240:]
    within = swap(jnp.concatenate([half(own, 8 - 8 * core), own[208:]], 0), chip, 1 - core)
    top = jnp.where(first, outside, within)
    bottom = jnp.where(first, within, outside)
    inside = jnp.stack([row != 0, row != n_row - 1]).astype(jnp.int32)
    return smooth(inside, own, top, bottom)


def solution(mesh):
    placed = (
        P("row", "col", None, None),
        P("row", "col", None),
        P("row", "col", None, None, None),
        P("row", "col", None, None),
        P("row", "col", None, None),
        P("row", "col", None, None),
        P("row", "col"),
        P("row", "col"),
    )
    return jax.shard_map(
        per_device, mesh=mesh, in_specs=placed, out_specs=P(None, "row", "col"), check_vma=False
    )
```

profile of v0, /device:TPU:6, one launch (start us, length us, event | category | flops | bytes accessed | tf_op | source)
XLA Modules:
  0.0 46.5 jit_solution(18014187302488079942)
XLA Ops:
  0.7 6.4 %shard_map.82 = (f32[38,8,128]{2,1,0:T(8,128)S(1)}, f32[38,8,128]{2,1,0:T(8,128)S(1)}, f32[3,208,128]{2,1,0:T(8,128)S(1)}) custom-call(s32[1]{0:T(128)} %bitcast.3.side_ref, s32[1]{0:T(128)} %bitcast.50.counts_in, s32[24]{0:T(128)} %bitcast.65, bf16[1,1,12,8192]{3,2,1,0:T(8,128)(2,1)} %ocean_in.1, s32[1,8192]{1,0:T(1,128)} %bitcast.64, ...), custom_call_target="tpu_custom_call" | custom-call | tf_op jit(solution)/shard_map/pallas_call | solution.py:203
  7.0 2.0 %all-gather = f32[76,8,128]{2,1,0:T(8,128)S(1)} all-gather(f32[38,8,128]{2,1,0:T(8,128)S(1)} %get-tuple-element.11), channel_id=2, replica_groups={{0,8},{1,9},{2,10},{3,11},{4,12},{5,13},{6,14},{7,15},{16,24},{17,25},{..., dimensions={0}, use_global_device_ids=true | all-gather | bytes 466944 | tf_op jit(solution)/shard_map/all_gather | solution.py:379
  9.1 4.2 %collective-permute-start = (f32[4,16,128]{2,1,0:T(8,128)S(1)}, f32[4,16,128]{2,1,0:T(8,128)S(1)}, u32[]{:S(2)}, u32[]{:S(2)}) collective-permute-start(f32[4,16,128]{2,1,0:T(8,128)S(1)} %get-tuple-element.25), channel_id=1, source_target_pairs={{0,10},{1,15},{2,12},{3,9},{4,14},{5,11},{6,8},{7,13},{8,6},{9,3},... | collective-permute-start | bytes 98312 | tf_op jit(solution)/shard_map/ppermute | solution.py:388
  13.4 0.1 pad_add_fusion.1.place_ref
  13.5 0.1 add_convert_fusion.inside_ref
  13.6 6.7 %all-gather.1 = f32[96,8,128]{2,1,0:T(8,128)S(1)} all-gather(f32[48,8,128]{2,1,0:T(8,128)S(1)} %pad_maximum_fusion), channel_id=3, replica_groups={{0,1},{2,3},{4,5},{6,7},{9,10},{11,12},{13,14},{15,8},{16,17},{18,19},{..., dimensions={0}, use_global_device_ids=true | all-gather | bytes 589824 | tf_op jit(solution)/shard_map/all_gather | solution.py:389
  20.2 0.0 collective-permute-done.far_ref
  20.2 1.4 %shard_map.83 = (f32[2,224,128]{2,1,0:T(8,128)S(1)}, f32[2,224,128]{2,1,0:T(8,128)S(1)}) custom-call(s32[2]{0:T(128)S(1)} %pad_add_fusion.1.place_ref, f32[2,48,8,128]{3,2,1,0:T(8,128)S(1)} %bitcast.51, f32[3,208,128]{2,1,0:T(8,128)S(1)} %get-tuple-element.12.mid_ref, f32[4,16,128]{2,1,0:T(8,128)S(1)} %collective-permute-done.far_ref, ...), custom_call_target="tpu_custom_call" | custom-call | tf_op jit(solution)/shard_map/pallas_call | solution.py:273
  21.6 3.5 %all-gather.2 = f32[4,224,128]{2,1,0:T(8,128)S(1)} all-gather(f32[2,224,128]{2,1,0:T(8,128)S(1)} %get-tuple-element.14), channel_id=4, replica_groups={{0,8},{1,9},{2,10},{3,11},{4,12},{5,13},{6,14},{7,15},{16,24},{17,25},{..., dimensions={0}, use_global_device_ids=true | all-gather | bytes 688128 | tf_op jit(solution)/shard_map/all_gather | solution.py:379
  25.4 16.9 %all-gather.3 = f32[752,128]{1,0:T(8,128)S(1)} all-gather(f32[376,128]{1,0:T(8,128)S(1)} %pad_maximum_fusion.1), channel_id=5, replica_groups={{8,16},{9,17},{10,18},{11,19},{12,20},{13,21},{14,22},{15,23},{24,32},{..., dimensions={0}, use_global_device_ids=true | all-gather | bytes 577536 | tf_op jit(solution)/shard_map/all_gather | solution.py:379
  42.4 1.9 %all-gather.4 = f32[272,128]{1,0:T(8,128)S(1)} all-gather(f32[136,128]{1,0:T(8,128)S(1)} %pad_maximum_fusion.2), channel_id=6, replica_groups={{0,8},{1,9},{2,10},{3,11},{4,12},{5,13},{6,14},{7,15},{16,24},{17,25},{..., dimensions={0}, use_global_device_ids=true | all-gather | bytes 208896 | tf_op jit(solution)/shard_map/all_gather | solution.py:379
  44.3 2.2 %shard_map.84 = f32[12,16,128]{2,1,0:T(8,128)} custom-call(s32[2]{0:T(128)S(1)} %add_convert_fusion.inside_ref, f32[240,128]{1,0:T(8,128)S(1)} %fusion.own_ref, f32[136,128]{1,0:T(8,128)S(1)} %get-tuple-element.20.top_ref, f32[136,128]{1,0:T(8,128)S(1)} %get-tuple-element.19.bottom_ref), custom_call_target="tpu_custom_call" | custom-call | tf_op jit(solution)/shard_map/pallas_call | solution.py:341
  (22 shorter events, 0.3 us)
Async XLA Ops:
  9.1 11.1 %collective-permute-start = (f32[4,16,128]{2,1,0:T(8,128)S(1)}, f32[4,16,128]{2,1,0:T(8,128)S(1)}, u32[]{:S(2)}, u32[]{:S(2)}) collective-permute-start(f32[4,16,128]{2,1,0:T(8,128)S(1)} %get-tuple-element.25), channel_id=1, source_target_pairs={{0,10},{1,15},{2,12},{3,9},{4,14},{5,11},{6,8},{7,13},{8,6},{9,3},... | collective-permute-start | bytes 98312 | tf_op jit(solution)/shard_map/ppermute | solution.py:388
where the time goes:
time: 47 us; the launch traced here: 46.5 us
  blocking collectives  31 us (66%)
  Pallas kernels  9.93 us (21%)
  starting transfers between devices  4.25 us (9%)
  between operations  0.82 us (2%)
    all_gather x4, blocking collectives, per_device(): lax.all_gather(value, both, axis_index_groups=groups)  24.4 us
    all_gather x1, blocking collectives, per_device(): lax.all_gather(jnp.concatenate([lower[:20], upper[:20], strips[:, 0:16].r...  6.65 us
    pallas_call x1, Pallas kernels, remap(): pl.pallas_call(functools.partial(remap_kernel, ga=ga, gb=gb), out_shape=(...  6.35 us
    ppermute x1, starting transfers between devices, per_device(): far = lax.ppermute(strips[:, 16:32], both, beyond)  4.25 us
    pallas_call x1, Pallas kernels, smooth(): pl.pallas_call(smooth_kernel, out_shape=jax.ShapeDtypeStruct((F, AY, AX),...  2.17 us
    pallas_call x1, Pallas kernels, collect(): pl.pallas_call(collect_kernel, out_shape=(half, half), in_specs=[pl.Block...  1.4 us
  transfers between devices with their start and end apart: 1, of which 0 were waited for; matrix products, arithmetic and copies ran while one was open for 0% of the time, Pallas kernels for 0%

commit v1 on v0

--- a/solution.py
+++ b/solution.py
@@ -8,7 +8,7 @@
 from jax.sharding import PartitionSpec as P
 
 F, AY, AX, OC, NBLK, BC, BR = 12, 16, 128, 8192, 24, 256, 128
-MIX = (1, 0)
+MIX = (0, 1)
 NT = (((1,), (1,)), ((), ()))
 
 
@@ -18,8 +18,8 @@
 
 
 def remap_kernel(side_ref, counts_in, dest_in, ocean_in, land_in, weights_in, col_in, row_in, kappa_in,
-                 sent_out, kept_out, mid_out, dest_ref, counts_ref, ocean_ref, land_ref, weight_ref, col_ref, row_ref, kappa_ref,
-                 fields_ref, table_ref, rows_ref, partial_ref, tiles_ref, raw_ref, strips_ref, extra_ref, used_ref, sems, out_sems, *, ga, gb):
+                 sent_ref, kept_ref, mid_ref, dest_ref, counts_ref, ocean_ref, land_ref, weight_ref, col_ref, row_ref, kappa_ref,
+                 fields_ref, table_ref, rows_ref, partial_ref, tiles_ref, raw_ref, strips_ref, used_ref, sems, *, ga, gb):
     f32, bf16, i32 = jnp.float32, jnp.bfloat16, jnp.int32
     pairs = ((land_in, land_ref), (ocean_in.at[0, 0], ocean_ref), (col_in.at[0, 0], col_ref), (weights_in.at[0, 0], weight_ref),
              (counts_in, counts_ref), (row_in.at[0, 0], row_ref), (dest_in, dest_ref), (kappa_in, kappa_ref))
@@ -39,8 +39,9 @@
     fields_ref[12:16, :] = jnp.zeros((4, OC), f32)
     low8 = fields_ref[8:16, :]
     down8 = pltpu.roll(low8, 4, 0)
-    blocks = OC // BC
-    cut = lambda a, h: a[:, h * BC:(h + 1) * BC]
+    deep = 512
+    blocks = OC // deep
+    cut = lambda a, h: a[:, h * deep:(h + 1) * deep]
     upper = fields_ref[0:8, :]
     rows_ref[0:8 * blocks, :] = jnp.concatenate([cut(upper, h) for h in range(blocks)], 0).astype(bf16)
     rows_ref[8 * blocks:12 * blocks, :] = jnp.concatenate(
@@ -57,14 +58,14 @@
         value = jnp.dot(picked, weight_ref[b], preferred_element_type=f32)
         partial_ref[b] = jnp.where(b < count, value, 0.0)
 
-    cells = lax.broadcasted_iota(i32, (BC, BC), 0)
+    cells = lax.broadcasted_iota(i32, (deep, BC), 0).astype(jnp.int16)
     odd2 = (lax.broadcasted_iota(i32, (8, BC), 0) >= 4).astype(i32)
 
     def pick_dot(b):
         col = col_ref[pl.ds(b, 1), :]
-        low = jnp.bitwise_and(col, BC - 1)
-        hi = jnp.right_shift(col, 8)
-        onehot = (cells == low).astype(f32).astype(bf16)
+        low = jnp.bitwise_and(col, deep - 1)
+        hi = jnp.right_shift(col, 9)
+        onehot = jnp.where(cells == jnp.broadcast_to(low, (deep, BC)).astype(jnp.int16), jnp.ones((), bf16), jnp.zeros((), bf16))
         got = jnp.dot(rows_ref[...], onehot, preferred_element_type=f32)
         hi8 = jnp.broadcast_to(hi, (8, BC))
         up = jnp.zeros((8, BC), f32)
@@ -151,31 +152,26 @@
     lax.fori_loop(0, NBLK // gb, place_group, 0)
 
     side = side_ref[0]
-    outs = []
-
-    def out(source, target):
-        outs.append(pltpu.make_async_copy(source, target, out_sems.at[len(outs)]))
-        outs[-1].start()
-
     main = F * AY
-    out(raw_ref.at[1 - side, pl.ds(0, 20)], sent_out.at[pl.ds(0, 20)])
-    out(raw_ref.at[side, pl.ds(0, 20)], kept_out.at[pl.ds(0, 20)])
-    out(tiles_ref.at[pl.ds(3, 3)], mid_out.at[:, 0:main])
+    for band in range(3):
+        mid_ref[band, 0:main] = tiles_ref[3 + band]
+        mid_ref[band, main:main + AY] = kappa_ref[...] if band == 1 else jnp.zeros((AY, AX), f32)
+    sent_ref[0:20] = raw_ref[1 - side, 0:20]
+    kept_ref[0:20] = raw_ref[side, 0:20]
     er = lax.broadcasted_iota(i32, (16, AX), 0)
     ec = lax.broadcasted_iota(i32, (16, AX), 1)
     edge = (ec == jnp.where(er < 8, er, er + AX - 16)).astype(f32).astype(bf16)
     edge2 = jnp.concatenate([edge, edge], 1)
     kappa = kappa_ref[...]
-    extra_ref[...] = jnp.zeros_like(extra_ref)
-    extra_ref[1] = kappa
-    out(extra_ref, mid_out.at[:, main:main + AY])
     for band in range(3):
         for dc in range(3):
             tile = jnp.concatenate([tiles_ref[3 * dc + band], kappa if 3 * dc + band == 4 else jnp.zeros((AY, AX), f32)], 0)
+            blank = jnp.zeros((128 - 13 * 8, AX), f32)
+            tile = jnp.concatenate([tile[AY * f:AY * f + 8] for f in range(13)] + [blank]
+                                   + [tile[AY * f + 8:AY * f + AY] for f in range(13)] + [blank], 0)
             hi, lo = split2(tile)
             strip = lax.dot_general(edge2, jnp.concatenate([hi, lo], 1), NT, preferred_element_type=f32)
-            first = strip[:, 0:128]
-            second = jnp.concatenate([strip[:, 128:], jnp.zeros((16, 256 - 13 * AY), f32)], 1)
+            first, second = strip[:, 0:128], strip[:, 128:256]
             west = (first[0:8], second[0:8])
             east = (first[8:16], second[8:16])
 
@@ -192,10 +188,8 @@
             else:
                 put(0, 2, west)
                 put(0, 4, east)
-    out(strips_ref.at[1 - side], sent_out.at[pl.ds(20, 18)])
-    out(strips_ref.at[side], kept_out.at[pl.ds(20, 18)])
-    for copy in outs:
-        copy.wait()
+    sent_ref[20:38] = strips_ref[1 - side]
+    kept_ref[20:38] = strips_ref[side]
 
 
 def remap(side, dest, counts, ocean, land, weights, col_map, row_map, kappa, ga=12, gb=24):
@@ -204,7 +198,7 @@
         functools.partial(remap_kernel, ga=ga, gb=gb),
         out_shape=(jax.ShapeDtypeStruct((38, 8, 128), f32), jax.ShapeDtypeStruct((38, 8, 128), f32), jax.ShapeDtypeStruct((3, 208, 128), f32)),
         in_specs=[pl.BlockSpec(memory_space=pltpu.SMEM)] + [pl.BlockSpec(memory_space=pltpu.HBM)] * 8,
-        out_specs=[pl.BlockSpec(memory_space=pl.ANY)] * 3,
+        out_specs=[pl.BlockSpec(memory_space=pltpu.VMEM)] * 3,
         scratch_shapes=[
             pltpu.SMEM((NBLK,), jnp.int32),
             pltpu.SMEM((1,), jnp.int32),
@@ -216,15 +210,13 @@
             pltpu.VMEM((AY, AX), f32),
             pltpu.VMEM((16, OC), f32),
             pltpu.VMEM((8, OC // 2), f32),
-            pltpu.VMEM((384, BC), jnp.bfloat16),
+            pltpu.VMEM((192, 512), jnp.bfloat16),
             pltpu.VMEM((NBLK, 16, BR), f32),
             pltpu.VMEM((9, F * AY, AX), f32),
             pltpu.VMEM((2, 22, 8, BR), f32),
             pltpu.VMEM((2, 18, 8, AX), f32),
-            pltpu.VMEM((3, AY, AX), f32),
             pltpu.SMEM((9,), jnp.int32),
             pltpu.SemaphoreType.DMA((8,)),
-            pltpu.SemaphoreType.DMA((6,)),
         ],
         compiler_params=pltpu.CompilerParams(vmem_limit_bytes=32 * 1024 * 1024),
     )(side, counts, *[pltpu.with_memory_space_constraint(v, pltpu.HBM) for v in (dest, ocean, land, weights, col_map, row_map, kappa)])
@@ -287,11 +279,10 @@
     f32, i32 = jnp.float32, jnp.int32
     wide = 2 * AX
     tall = AY + 16
-    strip = lambda ref, at: jnp.concatenate([ref[at:at + 8, :], ref[at + 8:at + 16, :]], 1)
-    below = lax.rem(lax.broadcasted_iota(i32, (8, wide), 1), AY) < 8
-    ends = lambda at: jnp.where(below, strip(bottom_ref, at), strip(top_ref, at))
-    for slot, (west, east) in enumerate(((strip(own_ref, 13 * AY), strip(own_ref, 13 * AY + 16)),
-                                         (ends(13 * 8), ends(13 * 8 + 16)))):
+    strip = lambda a, a_at, b, b_at: jnp.concatenate([a[a_at:a_at + 8, :], b[b_at:b_at + 8, :]], 1)
+    for slot, (west, east) in enumerate((
+            (strip(own_ref, 208, own_ref, 216), strip(own_ref, 224, own_ref, 232)),
+            (strip(bottom_ref, 104, top_ref, 104), strip(bottom_ref, 112, top_ref, 112)))):
         block = jnp.concatenate([east, jnp.zeros((AX - 16, wide), f32), west], 0)
         side_ref[slot, 0:AX] = block[:, :AX].T
         side_ref[slot, AX:wide] = block[:, AX:].T
@@ -305,9 +296,10 @@
         main_ref[f, 0:8] = keep(top_ref[8 * f:8 * f + 8], 0, 8)
         main_ref[f, 8:8 + AY] = own_ref[AY * f:AY * f + AY]
         main_ref[f, 8 + AY:tall] = keep(bottom_ref[8 * f:8 * f + 8], 8 + AY, tall)
-        halo_ref[f, 0:8] = keep(side_ref[1, AY * f + 8:AY * f + 16], 0, 8)
-        halo_ref[f, 8:8 + AY] = side_ref[0, AY * f:AY * f + AY]
-        halo_ref[f, 8 + AY:tall] = keep(side_ref[1, AY * f:AY * f + 8], 8 + AY, tall)
+        halo_ref[f, 0:8] = keep(side_ref[1, AX + 8 * f:AX + 8 * f + 8], 0, 8)
+        halo_ref[f, 8:16] = side_ref[0, 8 * f:8 * f + 8]
+        halo_ref[f, 16:24] = side_ref[0, AX + 8 * f:AX + 8 * f + 8]
+        halo_ref[f, 8 + AY:tall] = keep(side_ref[1, 8 * f:8 * f + 8], 8 + AY, tall)
 
     def lap(ref, f, lo, n, own_rolls, other_rolls):
         at = lambda by: ref[f, lo + by:lo + by + n]
@@ -397,13 +389,15 @@
     edges = jnp.concatenate([west, east], 1)
     mine_main, mine_edges = take(main, 1 - core), take(edges, 1 - core)
     out_main, out_edges = take(main, core), take(edges, core)
-    sent = jnp.concatenate([out_main, out_edges, half(mine_main, 8 * core), mine_edges], 0)
+    half_edges = lambda value, place: part(value.reshape(2, 2, 8, AX), place, 1, 1).reshape(16, AX)
+    main = F * AY
+    sent = jnp.concatenate([out_main[:main], out_edges, half(mine_main, 8 * core), half_edges(mine_edges, core)], 0)
     got = swap(sent, bands, core)
     outer = jnp.logical_or(row == 0, row == n_row - 1)
     got = jnp.where(outer, 0.0, got)
-    own = jnp.concatenate([mine_main, mine_edges], 0) + got[:240]
-    outside = jnp.concatenate([half(out_main, 8 - 8 * core), out_edges], 0) + got[240:]
-    within = swap(jnp.concatenate([half(own, 8 - 8 * core), own[208:]], 0), chip, 1 - core)
+    own = jnp.concatenate([mine_main[:main] + got[:main], mine_main[main:], mine_edges + got[main:main + 32]], 0)
+    outside = jnp.concatenate([half(out_main, 8 - 8 * core), half_edges(out_edges, 1 - core)], 0) + got[main + 32:]
+    within = swap(jnp.concatenate([half(own, 8 - 8 * core), half_edges(own[208:], 1 - core)], 0), chip, 1 - core)
     top = jnp.where(first, outside, within)
     bottom = jnp.where(first, within, outside)
     inside = jnp.stack([row != 0, row != n_row - 1]).astype(jnp.int32)

time: 47 us -> 46.4 us (0.987)
  Pallas kernels: 9.93 us -> 9.37 us
    pallas_call x1, Pallas kernels: 6.35 us -> 5.81 us  [remap(): pl.pallas_call(functools.partial(remap_kernel, ga=ga, gb=gb), out_shape=(...]
where the time goes in v1:
time: 46.4 us; the launch traced here: 45.8 us
  blocking collectives  30.8 us (66%)
  Pallas kernels  9.37 us (20%)
  starting transfers between devices  4.25 us (9%)
  between operations  0.86 us (2%)
    all_gather x4, blocking collectives, per_device(): lax.all_gather(value, both, axis_index_groups=groups)  24.2 us
    all_gather x1, blocking collectives, per_device(): lax.all_gather(jnp.concatenate([lower[:20], upper[:20], strips[:, 0:16].r...  6.65 us
    pallas_call x1, Pallas kernels, remap(): pl.pallas_call(functools.partial(remap_kernel, ga=ga, gb=gb), out_shape=(...  5.81 us
    ppermute x1, starting transfers between devices, per_device(): far = lax.ppermute(strips[:, 16:32], both, beyond)  4.25 us
    pallas_call x1, Pallas kernels, smooth(): pl.pallas_call(smooth_kernel, out_shape=jax.ShapeDtypeStruct((F, AY, AX),...  2.17 us
    pallas_call x1, Pallas kernels, collect(): pl.pallas_call(collect_kernel, out_shape=(half, half), in_specs=[pl.Block...  1.4 us
  transfers between devices with their start and end apart: 1, of which 0 were waited for; matrix products, arithmetic and copies ran while one was open for 0% of the time, Pallas kernels for 0%

profile of v1, /device:TPU:6, one launch (start us, length us, event | category | flops | bytes accessed | tf_op | source)
XLA Modules:
  0.0 45.8 jit_solution(14641939417024157460)
XLA Ops:
  0.7 5.8 %shard_map.82 = (f32[38,8,128]{2,1,0:T(8,128)S(1)}, f32[38,8,128]{2,1,0:T(8,128)S(1)}, f32[3,208,128]{2,1,0:T(8,128)S(1)}) custom-call(s32[1]{0:T(128)} %bitcast.3.side_ref, s32[1]{0:T(128)} %bitcast.57.counts_in, s32[24]{0:T(128)} %bitcast.75, bf16[1,1,12,8192]{3,2,1,0:T(8,128)(2,1)} %ocean_in.1, s32[1,8192]{1,0:T(1,128)} %bitcast.74, ...), custom_call_target="tpu_custom_call" | custom-call | tf_op jit(solution)/shard_map/pallas_call | solution.py:197
  6.5 2.0 %all-gather = f32[76,8,128]{2,1,0:T(8,128)S(1)} all-gather(f32[38,8,128]{2,1,0:T(8,128)S(1)} %get-tuple-element.11), channel_id=2, replica_groups={{0,8},{1,9},{2,10},{3,11},{4,12},{5,13},{6,14},{7,15},{16,24},{17,25},{..., dimensions={0}, use_global_device_ids=true | all-gather | bytes 466944 | tf_op jit(solution)/shard_map/all_gather | solution.py:371
  8.6 4.2 %collective-permute-start = (f32[4,16,128]{2,1,0:T(8,128)S(1)}, f32[4,16,128]{2,1,0:T(8,128)S(1)}, u32[]{:S(2)}, u32[]{:S(2)}) collective-permute-start(f32[4,16,128]{2,1,0:T(8,128)S(1)} %get-tuple-element.25), channel_id=1, source_target_pairs={{0,10},{1,15},{2,12},{3,9},{4,14},{5,11},{6,8},{7,13},{8,6},{9,3},... | collective-permute-start | bytes 98312 | tf_op jit(solution)/shard_map/ppermute | solution.py:380
  12.9 0.1 pad_add_fusion.1.place_ref
  12.9 0.1 add_convert_fusion.inside_ref
  13.0 6.7 %all-gather.1 = f32[96,8,128]{2,1,0:T(8,128)S(1)} all-gather(f32[48,8,128]{2,1,0:T(8,128)S(1)} %pad_maximum_fusion), channel_id=3, replica_groups={{0,1},{2,3},{4,5},{6,7},{9,10},{11,12},{13,14},{15,8},{16,17},{18,19},{..., dimensions={0}, use_global_device_ids=true | all-gather | bytes 589824 | tf_op jit(solution)/shard_map/all_gather | solution.py:381
  19.7 0.0 collective-permute-done.far_ref
  19.7 1.4 %shard_map.83 = (f32[2,224,128]{2,1,0:T(8,128)S(1)}, f32[2,224,128]{2,1,0:T(8,128)S(1)}) custom-call(s32[2]{0:T(128)S(1)} %pad_add_fusion.1.place_ref, f32[2,48,8,128]{3,2,1,0:T(8,128)S(1)} %bitcast.58, f32[3,208,128]{2,1,0:T(8,128)S(1)} %get-tuple-element.12.mid_ref, f32[4,16,128]{2,1,0:T(8,128)S(1)} %collective-permute-done.far_ref, ...), custom_call_target="tpu_custom_call" | custom-call | tf_op jit(solution)/shard_map/pallas_call | solution.py:265
  21.1 3.5 %all-gather.2 = f32[4,224,128]{2,1,0:T(8,128)S(1)} all-gather(f32[2,224,128]{2,1,0:T(8,128)S(1)} %get-tuple-element.14), channel_id=4, replica_groups={{0,8},{1,9},{2,10},{3,11},{4,12},{5,13},{6,14},{7,15},{16,24},{17,25},{..., dimensions={0}, use_global_device_ids=true | all-gather | bytes 688128 | tf_op jit(solution)/shard_map/all_gather | solution.py:371
  24.9 16.7 %all-gather.3 = f32[688,128]{1,0:T(8,128)S(1)} all-gather(f32[344,128]{1,0:T(8,128)S(1)} %pad_maximum_fusion.1), channel_id=5, replica_groups={{8,16},{9,17},{10,18},{11,19},{12,20},{13,21},{14,22},{15,23},{24,32},{..., dimensions={0}, use_global_device_ids=true | all-gather | bytes 528384 | tf_op jit(solution)/shard_map/all_gather | solution.py:371
  41.7 1.9 %all-gather.4 = f32[240,128]{1,0:T(8,128)S(1)} all-gather(f32[120,128]{1,0:T(8,128)S(1)} %pad_maximum_fusion.4), channel_id=6, replica_groups={{0,8},{1,9},{2,10},{3,11},{4,12},{5,13},{6,14},{7,15},{16,24},{17,25},{..., dimensions={0}, use_global_device_ids=true | all-gather | bytes 184320 | tf_op jit(solution)/shard_map/all_gather | solution.py:371
  43.7 2.2 %shard_map.84 = f32[12,16,128]{2,1,0:T(8,128)} custom-call(s32[2]{0:T(128)S(1)} %add_convert_fusion.inside_ref, f32[240,128]{1,0:T(8,128)S(1)} %pad_maximum_fusion.2.own_ref, f32[120,128]{1,0:T(8,128)S(1)} %get-tuple-element.20.top_ref, f32[120,128]{1,0:T(8,128)S(1)} %get-tuple-element.19.bottom_ref), custom_call_target="tpu_custom_call" | custom-call | tf_op jit(solution)/shard_map/pallas_call | solution.py:333
  (28 shorter events, 0.4 us)
Async XLA Ops:
  8.6 11.1 %collective-permute-start = (f32[4,16,128]{2,1,0:T(8,128)S(1)}, f32[4,16,128]{2,1,0:T(8,128)S(1)}, u32[]{:S(2)}, u32[]{:S(2)}) collective-permute-start(f32[4,16,128]{2,1,0:T(8,128)S(1)} %get-tuple-element.25), channel_id=1, source_target_pairs={{0,10},{1,15},{2,12},{3,9},{4,14},{5,11},{6,8},{7,13},{8,6},{9,3},... | collective-permute-start | bytes 98312 | tf_op jit(solution)/shard_map/ppermute | solution.py:380

commit v2 on v1

--- a/solution.py
+++ b/solution.py
@@ -8,7 +8,6 @@
 from jax.sharding import PartitionSpec as P
 
 F, AY, AX, OC, NBLK, BC, BR = 12, 16, 128, 8192, 24, 256, 128
-MIX = (0, 1)
 NT = (((1,), (1,)), ((), ()))
 
 
@@ -61,12 +60,14 @@
     cells = lax.broadcasted_iota(i32, (deep, BC), 0).astype(jnp.int16)
     odd2 = (lax.broadcasted_iota(i32, (8, BC), 0) >= 4).astype(i32)
 
-    def pick_dot(b):
+    def start_dot(b):
         col = col_ref[pl.ds(b, 1), :]
         low = jnp.bitwise_and(col, deep - 1)
         hi = jnp.right_shift(col, 9)
         onehot = jnp.where(cells == jnp.broadcast_to(low, (deep, BC)).astype(jnp.int16), jnp.ones((), bf16), jnp.zeros((), bf16))
-        got = jnp.dot(rows_ref[...], onehot, preferred_element_type=f32)
+        return hi, jnp.dot(rows_ref[...], onehot, preferred_element_type=f32)
+
+    def select_dot(b, hi, got):
         hi8 = jnp.broadcast_to(hi, (8, BC))
         up = jnp.zeros((8, BC), f32)
         for h in range(blocks):
@@ -101,8 +102,12 @@
 
     def groups(n, one):
         def step(i, carry):
-            for j in range(n):
-                (one if MIX[j % len(MIX)] else pick_dot)(i * n + j)
+            begun = [start_dot(i * n), start_dot(i * n + 2)]
+            for j in range(0, n, 2):
+                one(i * n + j + 1)
+                if j + 4 < n:
+                    begun.append(start_dot(i * n + j + 4))
+                select_dot(i * n + j, *begun.pop(0))
             return carry
         lax.fori_loop(0, NBLK // n, step, 0)
 

time: 46.4 us -> 45.7 us (0.985)
  Pallas kernels: 9.37 us -> 8.67 us
    pallas_call x1, Pallas kernels: 5.81 us -> 5.1 us  [remap(): pl.pallas_call(functools.partial(remap_kernel, ga=ga, gb=gb), out_shape=(...]
where the time goes in v2:
time: 45.7 us; the launch traced here: 45.1 us
  blocking collectives  30.8 us (67%)
  Pallas kernels  8.67 us (19%)
  starting transfers between devices  4.25 us (9%)
  between operations  0.86 us (2%)
    all_gather x4, blocking collectives, per_device(): lax.all_gather(value, both, axis_index_groups=groups)  24.2 us
    all_gather x1, blocking collectives, per_device(): lax.all_gather(jnp.concatenate([lower[:20], upper[:20], strips[:, 0:16].r...  6.65 us
    pallas_call x1, Pallas kernels, remap(): pl.pallas_call(functools.partial(remap_kernel, ga=ga, gb=gb), out_shape=(...  5.1 us
    ppermute x1, starting transfers between devices, per_device(): far = lax.ppermute(strips[:, 16:32], both, beyond)  4.25 us
    pallas_call x1, Pallas kernels, smooth(): pl.pallas_call(smooth_kernel, out_shape=jax.ShapeDtypeStruct((F, AY, AX),...  2.17 us
    pallas_call x1, Pallas kernels, collect(): pl.pallas_call(collect_kernel, out_shape=(half, half), in_specs=[pl.Block...  1.4 us
  transfers between devices with their start and end apart: 1, of which 0 were waited for; matrix products, arithmetic and copies ran while one was open for 0% of the time, Pallas kernels for 0%

profile of v2, /device:TPU:6, one launch (start us, length us, event | category | flops | bytes accessed | tf_op | source)
XLA Modules:
  0.0 45.1 jit_solution(3686635440287982041)
XLA Ops:
  0.7 5.1 %shard_map.82 = (f32[38,8,128]{2,1,0:T(8,128)S(1)}, f32[38,8,128]{2,1,0:T(8,128)S(1)}, f32[3,208,128]{2,1,0:T(8,128)S(1)}) custom-call(s32[1]{0:T(128)} %bitcast.3.side_ref, s32[1]{0:T(128)} %bitcast.57.counts_in, s32[24]{0:T(128)} %bitcast.75, bf16[1,1,12,8192]{3,2,1,0:T(8,128)(2,1)} %ocean_in.1, s32[1,8192]{1,0:T(1,128)} %bitcast.74, ...), custom_call_target="tpu_custom_call" | custom-call | tf_op jit(solution)/shard_map/pallas_call | solution.py:202
  5.8 2.0 %all-gather = f32[76,8,128]{2,1,0:T(8,128)S(1)} all-gather(f32[38,8,128]{2,1,0:T(8,128)S(1)} %get-tuple-element.11), channel_id=2, replica_groups={{0,8},{1,9},{2,10},{3,11},{4,12},{5,13},{6,14},{7,15},{16,24},{17,25},{..., dimensions={0}, use_global_device_ids=true | all-gather | bytes 466944 | tf_op jit(solution)/shard_map/all_gather | solution.py:376
  7.9 4.2 %collective-permute-start = (f32[4,16,128]{2,1,0:T(8,128)S(1)}, f32[4,16,128]{2,1,0:T(8,128)S(1)}, u32[]{:S(2)}, u32[]{:S(2)}) collective-permute-start(f32[4,16,128]{2,1,0:T(8,128)S(1)} %get-tuple-element.25), channel_id=1, source_target_pairs={{0,10},{1,15},{2,12},{3,9},{4,14},{5,11},{6,8},{7,13},{8,6},{9,3},... | collective-permute-start | bytes 98312 | tf_op jit(solution)/shard_map/ppermute | solution.py:385
  12.2 0.1 pad_add_fusion.1.place_ref
  12.2 0.1 add_convert_fusion.inside_ref
  12.3 6.7 %all-gather.1 = f32[96,8,128]{2,1,0:T(8,128)S(1)} all-gather(f32[48,8,128]{2,1,0:T(8,128)S(1)} %pad_maximum_fusion), channel_id=3, replica_groups={{0,1},{2,3},{4,5},{6,7},{9,10},{11,12},{13,14},{15,8},{16,17},{18,19},{..., dimensions={0}, use_global_device_ids=true | all-gather | bytes 589824 | tf_op jit(solution)/shard_map/all_gather | solution.py:386
  19.0 0.0 collective-permute-done.far_ref
  19.0 1.4 %shard_map.83 = (f32[2,224,128]{2,1,0:T(8,128)S(1)}, f32[2,224,128]{2,1,0:T(8,128)S(1)}) custom-call(s32[2]{0:T(128)S(1)} %pad_add_fusion.1.place_ref, f32[2,48,8,128]{3,2,1,0:T(8,128)S(1)} %bitcast.58, f32[3,208,128]{2,1,0:T(8,128)S(1)} %get-tuple-element.12.mid_ref, f32[4,16,128]{2,1,0:T(8,128)S(1)} %collective-permute-done.far_ref, ...), custom_call_target="tpu_custom_call" | custom-call | tf_op jit(solution)/shard_map/pallas_call | solution.py:270
  20.4 3.6 %all-gather.2 = f32[4,224,128]{2,1,0:T(8,128)S(1)} all-gather(f32[2,224,128]{2,1,0:T(8,128)S(1)} %get-tuple-element.14), channel_id=4, replica_groups={{0,8},{1,9},{2,10},{3,11},{4,12},{5,13},{6,14},{7,15},{16,24},{17,25},{..., dimensions={0}, use_global_device_ids=true | all-gather | bytes 688128 | tf_op jit(solution)/shard_map/all_gather | solution.py:376
  24.2 16.7 %all-gather.3 = f32[688,128]{1,0:T(8,128)S(1)} all-gather(f32[344,128]{1,0:T(8,128)S(1)} %pad_maximum_fusion.1), channel_id=5, replica_groups={{8,16},{9,17},{10,18},{11,19},{12,20},{13,21},{14,22},{15,23},{24,32},{..., dimensions={0}, use_global_device_ids=true | all-gather | bytes 528384 | tf_op jit(solution)/shard_map/all_gather | solution.py:376
  41.0 1.9 %all-gather.4 = f32[240,128]{1,0:T(8,128)S(1)} all-gather(f32[120,128]{1,0:T(8,128)S(1)} %pad_maximum_fusion.4), channel_id=6, replica_groups={{0,8},{1,9},{2,10},{3,11},{4,12},{5,13},{6,14},{7,15},{16,24},{17,25},{..., dimensions={0}, use_global_device_ids=true | all-gather | bytes 184320 | tf_op jit(solution)/shard_map/all_gather | solution.py:376
  43.0 2.2 %shard_map.84 = f32[12,16,128]{2,1,0:T(8,128)} custom-call(s32[2]{0:T(128)S(1)} %add_convert_fusion.inside_ref, f32[240,128]{1,0:T(8,128)S(1)} %pad_maximum_fusion.2.own_ref, f32[120,128]{1,0:T(8,128)S(1)} %get-tuple-element.20.top_ref, f32[120,128]{1,0:T(8,128)S(1)} %get-tuple-element.19.bottom_ref), custom_call_target="tpu_custom_call" | custom-call | tf_op jit(solution)/shard_map/pallas_call | solution.py:338
  (28 shorter events, 0.4 us)
Async XLA Ops:
  7.9 11.1 %collective-permute-start = (f32[4,16,128]{2,1,0:T(8,128)S(1)}, f32[4,16,128]{2,1,0:T(8,128)S(1)}, u32[]{:S(2)}, u32[]{:S(2)}) collective-permute-start(f32[4,16,128]{2,1,0:T(8,128)S(1)} %get-tuple-element.25), channel_id=1, source_target_pairs={{0,10},{1,15},{2,12},{3,9},{4,14},{5,11},{6,8},{7,13},{8,6},{9,3},... | collective-permute-start | bytes 98312 | tf_op jit(solution)/shard_map/ppermute | solution.py:385

commit v3 on v2

--- a/solution.py
+++ b/solution.py
@@ -156,7 +156,7 @@
 
     lax.fori_loop(0, NBLK // gb, place_group, 0)
 
-    side = side_ref[0]
+    side = side_ref[1]
     main = F * AY
     for band in range(3):
         mid_ref[band, 0:main] = tiles_ref[3 + band]
@@ -294,8 +294,8 @@
 
     rows = lax.broadcasted_iota(i32, (tall, AX), 0)
     lane = lax.broadcasted_iota(i32, (24, AX), 1)
-    inside = jnp.logical_and(jnp.logical_or(rows >= 8, inside_ref[0] == 1),
-                             jnp.logical_or(rows < 8 + AY, inside_ref[1] == 1))
+    inside = jnp.logical_and(jnp.logical_or(rows >= 8, inside_ref[2] == 1),
+                             jnp.logical_or(rows < 8 + AY, inside_ref[3] == 1))
     for f in range(F + 1):
         keep = (lambda v, lo, hi: jnp.where(inside[lo:hi], v, 0.0)) if f < F else (lambda v, lo, hi: v)
         main_ref[f, 0:8] = keep(top_ref[8 * f:8 * f + 8], 0, 8)
@@ -372,12 +372,13 @@
     first = core == 0
     ahead = (row + col) % 2 == 0
     side = jnp.where(ahead, 1, 0).astype(jnp.int32)
+    place = jnp.stack([v.astype(jnp.int32) for v in (core, side, row != 0, row != n_row - 1)])
     swap = lambda value, groups, place: lax.dynamic_index_in_dim(
         lax.all_gather(value, both, axis_index_groups=groups), place, 0, keepdims=False)
     take = lambda value, place: lax.dynamic_index_in_dim(value, place, 0, keepdims=False)
     part = lambda value, start, size, dim: lax.dynamic_slice_in_dim(value, start, size, dim)
 
-    sent, mine, mid = remap(side.reshape(1), dest.reshape(NBLK), counts.reshape(1), ocean, land.reshape(1, OC), weights, col_map, row_map, kappa)
+    sent, mine, mid = remap(place, dest.reshape(NBLK), counts.reshape(1), ocean, land.reshape(1, OC), weights, col_map, row_map, kappa)
     other = swap(sent, chip, 1 - core)
     lower, upper = jnp.where(first, mine, other), jnp.where(first, other, mine)
     lift = lambda value, before: jnp.pad(value[20:].reshape(3, 48, AX), ((before, 1 - before), (0, 0), (0, 0)))
@@ -385,7 +386,7 @@
     far = lax.ppermute(strips[:, 16:32], both, beyond)
     near = lax.all_gather(jnp.concatenate([lower[:20], upper[:20], strips[:, 0:16].reshape(8, 8, AX)], 0),
                           both, axis_index_groups=beside)
-    sent, mine = collect(jnp.stack([core, side]).astype(jnp.int32), near, mid, far, strips[:, 32:48])
+    sent, mine = collect(place, near, mid, far, strips[:, 32:48])
     other = swap(sent, chip, 1 - core)
     east = jnp.where(ahead, mine[:, 208:], other[:, 208:])
     west = jnp.where(ahead, other[:, 208:], mine[:, 208:])
@@ -405,8 +406,7 @@
     within = swap(jnp.concatenate([half(own, 8 - 8 * core), half_edges(own[208:], 1 - core)], 0), chip, 1 - core)
     top = jnp.where(first, outside, within)
     bottom = jnp.where(first, within, outside)
-    inside = jnp.stack([row != 0, row != n_row - 1]).astype(jnp.int32)
-    return smooth(inside, own, top, bottom)
+    return smooth(place, own, top, bottom)
 
 
 def solution(mesh):

time: 45.7 us -> 46.1 us (level)
  Pallas kernels: 8.67 us -> 9.21 us
    pallas_call x1, Pallas kernels: 5.1 us -> 5.64 us  [remap(): pl.pallas_call(functools.partial(remap_kernel, ga=ga, gb=gb), out_shape=(...]
where the time goes in v3:
time: 46.1 us; the launch traced here: 45.6 us
  blocking collectives  30.8 us (67%)
  Pallas kernels  9.21 us (20%)
  starting transfers between devices  4.25 us (9%)
  between operations  0.87 us (2%)
    all_gather x4, blocking collectives, per_device(): lax.all_gather(value, both, axis_index_groups=groups)  24.2 us
    all_gather x1, blocking collectives, per_device(): lax.all_gather(jnp.concatenate([lower[:20], upper[:20], strips[:, 0:16].r...  6.65 us
    pallas_call x1, Pallas kernels, remap(): pl.pallas_call(functools.partial(remap_kernel, ga=ga, gb=gb), out_shape=(...  5.64 us
    ppermute x1, starting transfers between devices, per_device(): far = lax.ppermute(strips[:, 16:32], both, beyond)  4.25 us
    pallas_call x1, Pallas kernels, smooth(): pl.pallas_call(smooth_kernel, out_shape=jax.ShapeDtypeStruct((F, AY, AX),...  2.17 us
    pallas_call x1, Pallas kernels, collect(): pl.pallas_call(collect_kernel, out_shape=(half, half), in_specs=[pl.Block...  1.4 us
  transfers between devices with their start and end apart: 1, of which 0 were waited for; matrix products, arithmetic and copies ran while one was open for 0% of the time, Pallas kernels for 0%

profile of v3, /device:TPU:6, one launch (start us, length us, event | category | flops | bytes accessed | tf_op | source)
XLA Modules:
  0.0 45.6 jit_solution(14038167599083624929)
XLA Ops:
  0.7 0.1 pad_add_fusion.1.side_ref.place_ref.inside_ref
  0.7 5.6 %shard_map.82 = (f32[38,8,128]{2,1,0:T(8,128)S(1)}, f32[38,8,128]{2,1,0:T(8,128)S(1)}, f32[3,208,128]{2,1,0:T(8,128)S(1)}) custom-call(s32[4]{0:T(128)S(1)} %pad_add_fusion.1.side_ref.place_ref.inside_ref, s32[1]{0:T(128)} %bitcast.57.counts_in, s32[24]{0:T(128)} %bitcast.75, bf16[1,1,12,8192]{3,2,1,0:T(8,128)(2,1)} %ocean_in.1, s32[1,8192]{1,0:T(1,128)} %bitcast.74, ...), custom_call_target="tpu_custom_call" | custom-call | tf_op jit(solution)/shard_map/pallas_call | solution.py:202
  6.4 2.0 %all-gather = f32[76,8,128]{2,1,0:T(8,128)S(1)} all-gather(f32[38,8,128]{2,1,0:T(8,128)S(1)} %get-tuple-element.11), channel_id=2, replica_groups={{0,8},{1,9},{2,10},{3,11},{4,12},{5,13},{6,14},{7,15},{16,24},{17,25},{..., dimensions={0}, use_global_device_ids=true | all-gather | bytes 466944 | tf_op jit(solution)/shard_map/all_gather | solution.py:377
  8.5 4.3 %collective-permute-start = (f32[4,16,128]{2,1,0:T(8,128)S(1)}, f32[4,16,128]{2,1,0:T(8,128)S(1)}, u32[]{:S(2)}, u32[]{:S(2)}) collective-permute-start(f32[4,16,128]{2,1,0:T(8,128)S(1)} %get-tuple-element.25), channel_id=1, source_target_pairs={{0,10},{1,15},{2,12},{3,9},{4,14},{5,11},{6,8},{7,13},{8,6},{9,3},... | collective-permute-start | bytes 98312 | tf_op jit(solution)/shard_map/ppermute | solution.py:386
  12.8 6.7 %all-gather.1 = f32[96,8,128]{2,1,0:T(8,128)S(1)} all-gather(f32[48,8,128]{2,1,0:T(8,128)S(1)} %pad_maximum_fusion), channel_id=3, replica_groups={{0,1},{2,3},{4,5},{6,7},{9,10},{11,12},{13,14},{15,8},{16,17},{18,19},{..., dimensions={0}, use_global_device_ids=true | all-gather | bytes 589824 | tf_op jit(solution)/shard_map/all_gather | solution.py:387
  19.5 0.0 collective-permute-done.far_ref
  19.5 1.4 %shard_map.83 = (f32[2,224,128]{2,1,0:T(8,128)S(1)}, f32[2,224,128]{2,1,0:T(8,128)S(1)}) custom-call(s32[4]{0:T(128)S(1)} %pad_add_fusion.1.side_ref.place_ref.inside_ref, f32[2,48,8,128]{3,2,1,0:T(8,128)S(1)} %bitcast.58, f32[3,208,128]{2,1,0:T(8,128)S(1)} %get-tuple-element.12.mid_ref, f32[4,16,128]{2,1,0:T(8,128)S(1)} %collective-permute-done.far_ref, ...), custom_call_target="tpu_custom_call" | custom-call | tf_op jit(solution)/shard_map/pallas_call | solution.py:270
  20.9 3.5 %all-gather.2 = f32[4,224,128]{2,1,0:T(8,128)S(1)} all-gather(f32[2,224,128]{2,1,0:T(8,128)S(1)} %get-tuple-element.14), channel_id=4, replica_groups={{0,8},{1,9},{2,10},{3,11},{4,12},{5,13},{6,14},{7,15},{16,24},{17,25},{..., dimensions={0}, use_global_device_ids=true | all-gather | bytes 688128 | tf_op jit(solution)/shard_map/all_gather | solution.py:377
  24.6 16.7 %all-gather.3 = f32[688,128]{1,0:T(8,128)S(1)} all-gather(f32[344,128]{1,0:T(8,128)S(1)} %pad_maximum_fusion.1), channel_id=5, replica_groups={{8,16},{9,17},{10,18},{11,19},{12,20},{13,21},{14,22},{15,23},{24,32},{..., dimensions={0}, use_global_device_ids=true | all-gather | bytes 528384 | tf_op jit(solution)/shard_map/all_gather | solution.py:377
  41.5 1.9 %all-gather.4 = f32[240,128]{1,0:T(8,128)S(1)} all-gather(f32[120,128]{1,0:T(8,128)S(1)} %pad_maximum_fusion.4), channel_id=6, replica_groups={{0,8},{1,9},{2,10},{3,11},{4,12},{5,13},{6,14},{7,15},{16,24},{17,25},{..., dimensions={0}, use_global_device_ids=true | all-gather | bytes 184320 | tf_op jit(solution)/shard_map/all_gather | solution.py:377
  43.4 2.2 %shard_map.84 = f32[12,16,128]{2,1,0:T(8,128)} custom-call(s32[4]{0:T(128)S(1)} %pad_add_fusion.1.side_ref.place_ref.inside_ref, f32[240,128]{1,0:T(8,128)S(1)} %pad_maximum_fusion.2.own_ref, f32[120,128]{1,0:T(8,128)S(1)} %get-tuple-element.20.top_ref, f32[120,128]{1,0:T(8,128)S(1)} %get-tuple-element.19.bottom_ref), custom_call_target="tpu_custom_call" | custom-call | tf_op jit(solution)/shard_map/pallas_call | solution.py:338
  (28 shorter events, 0.4 us)
Async XLA Ops:
  8.5 11.0 %collective-permute-start = (f32[4,16,128]{2,1,0:T(8,128)S(1)}, f32[4,16,128]{2,1,0:T(8,128)S(1)}, u32[]{:S(2)}, u32[]{:S(2)}) collective-permute-start(f32[4,16,128]{2,1,0:T(8,128)S(1)} %get-tuple-element.25), channel_id=1, source_target_pairs={{0,10},{1,15},{2,12},{3,9},{4,14},{5,11},{6,8},{7,13},{8,6},{9,3},... | collective-permute-start | bytes 98312 | tf_op jit(solution)/shard_map/ppermute | solution.py:386
